TPU v7x, 32 devices: a whole 2x2x4 slice. The times are simulated.
32 devices in a mesh: cell: 2 (over x), blk: 16 (over z, y, core).
Axes of the slice: x: 2, y: 2, z: 4, core: 2. Of those that a mesh axis runs over, the one named last changes fastest.
Arguments:
- psi_val: float32 [256, 64, 64, 64], P('cell', 'blk'), parts along dimension 0, may hold values from -6 to 6
- psi_cond: float32 [6, 64, 64, 64], P('cell', 'blk'), parts along dimension 0, may hold values from -6 to 6
- e_val: float32 [256], P('cell'), parts along dimension 0, may hold values from -8 to -1
- e_cond: float32 [6], P('cell'), parts along dimension 0, may hold values from 1 to 8
- occ: int32 [256], P('cell'), parts along dimension 0, may hold values from 1 to 2
- freq: float32 [10], P('cell'), parts along dimension 0, may hold values from 0.5 to 16
- gmap: int32 [8192], P('cell'), parts along dimension 0, may hold values from 0 to 262143, as said below
Outputs:
- chi_real: float32 [10, 4096, 4096], P('cell', 'blk'), parts along dimension 0
- chi_imag: float32 [10, 4096, 4096], P('cell', 'blk'), parts along dimension 0
There are 2 independent parts, one for each index of `cell`. A program takes and returns all parts, laid end to end along the dimension named above; each array names one. Nothing has to cross between parts.
Inputs may be any that keep to these rules, and one draw needn't show every extreme that they name: `gmap`: the 4096 indices are distinct; index 0 and index 262143 are always among them.
All inputs are finite; a program needn't handle non-finite values.
Results may differ from a plain program's by a relative error of at most 0.0001.
Values sent between devices are 32-bit elements; how exact they have to be, the bound alone decides.
A program may use at most 256 MiB of HBM per device.

v0:
```python
import math

import jax
import jax.numpy as jnp
from jax import lax
from jax.sharding import PartitionSpec as P

highest = lax.Precision.HIGHEST


def dft_tables(length):
    counter = jnp.arange(length, dtype=jnp.int32)
    angles = (counter[:, None] * counter[None, :] % length).astype(jnp.float32) * (
        2.0 * math.pi / length
    )
    return (jnp.cos(angles), jnp.sin(angles))


def plane_picks(val_part, cond_part, column_idx):
    num_val, planes, size_y, size_z = val_part.shape
    num_cond = cond_part.shape[0]
    pair_count = num_val * num_cond
    density = (val_part[:, None] * cond_part[None]).reshape(pair_count, planes, size_y, size_z)
    cos_z, sin_z = dft_tables(size_z)
    real_a = jnp.einsum("pxyz,zk->ykxp", density, cos_z, precision=highest)
    imag_a = -jnp.einsum("pxyz,zk->ykxp", density, sin_z, precision=highest)
    cos_y, sin_y = dft_tables(size_y)
    real_b = jnp.einsum("ly,ykxp->lkxp", cos_y, real_a, precision=highest) + jnp.einsum(
        "ly,ykxp->lkxp", sin_y, imag_a, precision=highest
    )
    imag_b = jnp.einsum("ly,ykxp->lkxp", cos_y, imag_a, precision=highest) - jnp.einsum(
        "ly,ykxp->lkxp", sin_y, real_a, precision=highest
    )
    return jnp.concatenate(
        [
            jnp.take(real_b.reshape(size_y * size_z, planes, pair_count), column_idx, axis=0),
            jnp.take(imag_b.reshape(size_y * size_z, planes, pair_count), column_idx, axis=0),
        ],
        axis=2,
    )


def phase_sum(values, freq_x, positions, size_x, norm_factor):
    half = values.shape[2] // 2
    angles = (freq_x[:, None] * positions[None, :] % size_x).astype(jnp.float32) * (
        2.0 * math.pi / size_x
    )
    cosine = jnp.cos(angles)[:, :, None]
    sine = jnp.sin(angles)[:, :, None]
    real_v = values[:, :, :half]
    imag_v = values[:, :, half:]
    real_m = jnp.sum(real_v * cosine + imag_v * sine, axis=1)
    imag_m = jnp.sum(imag_v * cosine - real_v * sine, axis=1)
    return jnp.concatenate([real_m, imag_m], axis=1) * norm_factor


def body(psi_val, psi_cond, e_val, e_cond, occ, freq, gmap):
    num_val, planes, size_y, size_z = psi_val.shape
    num_cond = psi_cond.shape[0]
    pairs = num_val * num_cond
    devices_blk = lax.axis_size("blk")
    size_x = planes * devices_blk
    total_points = size_x * size_y * size_z
    norm_factor = 1.0 / math.sqrt(total_points)
    column_idx = gmap % (size_y * size_z)
    plane_freq = gmap // (size_y * size_z)
    picked = plane_picks(psi_val, psi_cond, column_idx)
    positions = lax.axis_index("blk") * planes + jnp.arange(planes, dtype=jnp.int32)
    owned = lax.psum_scatter(
        phase_sum(picked, plane_freq, positions, size_x, norm_factor),
        "blk",
        scatter_dimension=0,
        tiled=True,
    )
    gaps = e_val[:, None] - e_cond[None, :]
    occ_col = occ.astype(jnp.float32)[:, None, None]
    weights = (
        occ_col
        * gaps[:, :, None]
        / (gaps[:, :, None] * gaps[:, :, None] + (freq * freq)[None, None, :])
    )
    weights = weights.reshape(pairs, freq.shape[0]) / math.sqrt(pairs)
    freq_weights = jnp.transpose(weights)[:, None, :]
    real_w = owned[None, :, :pairs] * freq_weights
    imag_w = owned[None, :, pairs:] * freq_weights
    left_side = jnp.stack(
        [jnp.concatenate([real_w, imag_w], axis=2), jnp.concatenate([imag_w, -real_w], axis=2)],
        axis=0,
    )
    chi_both = jnp.einsum(
        "awgk,hk->awgh",
        left_side,
        lax.all_gather(owned, "blk", axis=0, tiled=True),
        precision=highest,
    )
    return (chi_both[0], chi_both[1])


def solution(mesh):
    return jax.shard_map(
        body,
        mesh=mesh,
        in_specs=(
            P("cell", "blk", None, None),
            P("cell", "blk", None, None),
            P("cell"),
            P("cell"),
            P("cell"),
            P("cell"),
            P("cell"),
        ),
        out_specs=(P("cell", "blk", None), P("cell", "blk", None)),
        check_vma=False,
    )
```

profile of v0, /device:TPU:0, one launch (start us, length us, event | category | flops | bytes accessed | tf_op | source)
XLA Modules:
  0.0 1110.6 jit_solution(17548782149290452893)
XLA Ops:
  7.2 16.3 %copy.40 = f32[128,4,64,64]{3,2,1,0:T(8,128)} copy(f32[128,4,64,64]{0,3,2,1:T(8,128)} %param.9) | data formatting | bytes 16777216 | tf_op args[0]
  23.5 23.2 %broadcast_multiply_fusion = f32[128,3,4,64,64]{4,3,2,1,0:T(8,128)} fusion(f32[3,4,64,64]{3,2,1,0:T(8,128)S(1)} %copy-done, f32[128,4,64,64]{3,2,1,0:T(8,128)} %copy.40), kind=kLoop, calls=%fused_computation.5 | loop fusion | flops 6291456 | bytes 33751040 | tf_op jit(solution)/shard_map/mul | solution.py:23
  46.7 40.4 %copy.42 = f32[384,4,64,64]{0,3,2,1:T(8,128)} copy(f32[384,4,64,64]{3,2,1,0:T(8,128)} %bitcast.45) | data formatting | bytes 50331648 | tf_op jit(solution)/shard_map/mul | solution.py:23
  87.1 29.5 %negate_bitcast_fusion = f32[64,64,4,384]{3,1,0,2:T(8,128)} fusion(f32[384,4,64,64]{0,3,2,1:T(8,128)} %copy.42), kind=kOutput, calls=%fused_computation.4 | convolution fusion | flops 4838187008 | bytes 50331648 | tf_op jit(solution)/shard_map/pxyz,zk->ykxp/dot_general | solution.py:26
  116.6 29.9 %convolution_bitcast_fusion = f32[64,64,4,384]{3,1,0,2:T(8,128)} fusion(f32[384,4,64,64]{0,3,2,1:T(8,128)} %copy.42), kind=kOutput, calls=%fused_computation.19 | convolution fusion | flops 4831895552 | bytes 50331648 | tf_op jit(solution)/shard_map/pxyz,zk->ykxp/dot_general | solution.py:25
  146.6 52.3 %fusion.2 = f32[64,64,4,384]{3,0,2,1:T(8,128)} fusion(f32[64,64,4,384]{3,1,0,2:T(8,128)} %negate_bitcast_fusion), kind=kOutput, calls=%fused_computation.8 | convolution fusion | flops 4831895552 | bytes 50331648 | tf_op jit(solution)/shard_map/ly,ykxp->lkxp/dot_general | solution.py:28
  198.9 51.7 %fusion = f32[64,64,4,384]{3,0,2,1:T(8,128)} fusion(f32[64,64,4,384]{3,1,0,2:T(8,128)} %negate_bitcast_fusion), kind=kOutput, calls=%fused_computation.6 | convolution fusion | flops 4831895552 | bytes 50331648 | tf_op jit(solution)/shard_map/ly,ykxp->lkxp/dot_general | solution.py:31
  250.7 54.9 %fusion.10 = f32[64,64,4,384]{3,0,2,1:T(8,128)} fusion(f32[64,64,4,384]{3,0,2,1:T(8,128)} %fusion.2, f32[64,64,4,384]{3,1,0,2:T(8,128)} %convolution_bitcast_fusion), kind=kOutput, calls=%fused_computation.20 | convolution fusion | flops 4838187008 | bytes 75497472 | tf_op jit(solution)/shard_map/ly,ykxp->lkxp/dot_general | solution.py:28
  305.7 21.8 %copy.47 = f32[64,64,4,384]{3,1,0,2:T(8,128)S(1)} copy(f32[64,64,4,384]{3,0,2,1:T(8,128)} %fusion.10) | data formatting | bytes 50331648 | tf_op jit(solution)/shard_map/add | solution.py:28
  327.5 59.9 %copy.48 = f32[4096,4,384]{2,1,0:T(4,128)} copy(f32[4096,4,384]{2,0,1:T(8,128)S(1)} %bitcast.46) | data formatting | bytes 50331648 | tf_op jit(solution)/shard_map/reshape | solution.py:36
  387.3 54.7 %fusion.13 = f32[64,64,4,384]{3,0,2,1:T(8,128)} fusion(f32[64,64,4,384]{3,0,2,1:T(8,128)} %fusion, f32[64,64,4,384]{3,1,0,2:T(8,128)} %convolution_bitcast_fusion), kind=kOutput, calls=%fused_computation.21 | convolution fusion | flops 4838187008 | bytes 75497472 | tf_op jit(solution)/shard_map/ly,ykxp->lkxp/dot_general | solution.py:31
  442.0 21.8 %copy.52 = f32[64,64,4,384]{3,1,0,2:T(8,128)S(1)} copy(f32[64,64,4,384]{3,0,2,1:T(8,128)} %fusion.13) | data formatting | bytes 50331648 | tf_op jit(solution)/shard_map/sub | solution.py:31
  463.8 59.8 %copy.53 = f32[4096,4,384]{2,1,0:T(4,128)} copy(f32[4096,4,384]{2,0,1:T(8,128)S(1)} %bitcast.47) | data formatting | bytes 50331648 | tf_op jit(solution)/shard_map/reshape | solution.py:37
  523.7 53.5 %gather_fusion = f32[4096,4,384]{2,1,0:T(4,128)} fusion(f32[4096,4,384]{2,1,0:T(4,128)} %copy.48, s32[4096]{0:T(1024)S(1)} %get-tuple-element.16), kind=kCustom, calls=%fused_computation.clone | custom fusion | bytes 50348032 | tf_op jit(solution)/shard_map/jit(_take)/gather | solution.py:36
  577.2 53.5 %gather_fusion.1 = f32[4096,4,384]{2,1,0:T(4,128)} fusion(f32[4096,4,384]{2,1,0:T(4,128)} %copy.53, s32[4096]{0:T(1024)S(1)} %get-tuple-element.16), kind=kCustom, calls=%fused_computation.1.clone | custom fusion | bytes 50348032 | tf_op jit(solution)/shard_map/jit(_take)/gather | solution.py:37
  630.7 0.6 fusion.33
  631.3 0.6 copy.49
  632.0 2.0 copy.54
  633.9 82.4 %add_reduce_fusion = (f32[4096,384]{1,0:T(8,128)}, f32[4096,384]{1,0:T(8,128)}) fusion(f32[4096,4,384]{2,1,0:T(4,128)} %gather_fusion.1, f32[4096,4,384]{2,1,0:T(4,128)} %gather_fusion, f32[4096,4]{1,0:T(8,128)} %copy.54, f32[4096,4]{1,0:T(8,128)S(1)} %copy.49, pred[4096]{0:T(1024)(128)(4,1)S(1)} %compare_and_fusion), kind=kLoop, calls=%fused_computation.3 | loop fusion | flops 59768832 | bytes 63049728 | tf_op jit(solution)/shard_map/reduce_sum | solution.py:52
  716.4 10.3 maximum_multiply_fusion
  726.8 137.4 %reduce-scatter.2.cloned.1.call-done = f32[256,768]{1,0:T(8,128)} async-done(((f32[4096,768]{1,0:T(8,128)}), f32[256,768]{1,0:T(8,128)}) %reduce-scatter.2.cloned.1.call-update) | async-done | bytes 786448 | tf_op jit(solution)/shard_map/reduce_scatter | solution.py:69
  864.2 0.1 mul.224
  864.3 0.2 mul.225
  864.6 0.2 sub.40
  864.9 0.2 sub.42
  865.1 0.1 divide_multiply_fusion
  865.2 1.2 fusion.72
  866.3 0.5 broadcast_multiply_fusion.2
  866.9 3.9 maximum_bitcast_fusion
  870.8 95.6 %all-gather.2.cloned.1.call-done = f32[4096,768]{1,0:T(8,128)} async-done(((f32[256,768]{1,0:T(8,128)}), f32[4096,768]{1,0:T(8,128)}) %all-gather.2.cloned.1.call-update) | async-done | bytes 12582928 | tf_op jit(solution)/shard_map/all_gather | solution.py:93
  966.4 108.3 %fusion.8 = f32[2,5,256,4096]{3,2,1,0:T(8,128)} fusion(f32[4096,768]{1,0:T(8,128)} %all-gather.2.cloned.1.call-done, f32[1,5,256,768]{3,2,1,0:T(8,128)} %get-tuple-element.8, f32[1,5,256,768]{3,2,1,0:T(8,128)} %get-tuple-element.7), kind=kOutput, calls=%fused_computation.17 | convolution fusion | flops 96638730240 | bytes 62390272 | tf_op jit(solution)/shard_map/awgk,hk->awgh/dot_general | solution.py:90
  1074.7 28.8 %slice_bitcast_fusion = (f32[5,256,4096]{2,1,0:T(8,128)}, f32[5,256,4096]{2,1,0:T(8,128)}) fusion(f32[2,5,256,4096]{3,2,1,0:T(8,128)} %fusion.8), kind=kLoop, calls=%fused_computation.14 | loop fusion | bytes 83886080 | tf_op jit(solution)/shard_map/squeeze | solution.py:96
  (24 shorter events, 0.3 us)
Async XLA Ops:
  7.2 16.3 %copy-start = (f32[3,4,64,64]{3,2,1,0:T(8,128)S(1)}, f32[3,4,64,64]{3,2,1,0:T(8,128)}, u32[]{:S(2)}) copy-start(f32[3,4,64,64]{3,2,1,0:T(8,128)} %param.10) | copy-start | bytes 589828
  7.2 857.0 %reduce-scatter.2.cloned.1.call-start = ((), (), s32[]{:S(2)}) async-start(), calls=%async_computation.1 | async-start | bytes 13369344 | tf_op jit(solution)/shard_map/reduce_scatter | solution.py:69
  198.9 51.8 %copy-start.1 = (s32[4096]{0:T(1024)S(1)}, s32[4096]{0:T(1024)}, u32[]{:S(2)}) copy-start(s32[4096]{0:T(1024)} %param.15) | copy-start | bytes 49156
  716.4 147.9 %copy-start.4 = (s32[128]{0:T(128)S(1)}, s32[128]{0:T(128)}, u32[]{:S(2)}) copy-start(s32[128]{0:T(128)} %param.13) | copy-start | bytes 1540
  716.4 148.2 %copy-start.2 = (f32[128]{0:T(128)S(1)}, f32[128]{0:T(128)}, u32[]{:S(2)}) copy-start(f32[128]{0:T(128)} %param.11) | copy-start | bytes 1540
  716.4 148.5 %copy-start.3 = (f32[3]{0:T(128)S(1)}, f32[3]{0:T(128)}, u32[]{:S(2)}) copy-start(f32[3]{0:T(128)} %param.12) | copy-start | bytes 40
  716.4 148.7 %copy-start.5 = (f32[5]{0:T(128)S(1)}, f32[5]{0:T(128)}, u32[]{:S(2)}) copy-start(f32[5]{0:T(128)} %param.14) | copy-start | bytes 64
  726.7 239.7 %all-gather.2.cloned.1.call-start = ((), (), s32[]{:S(2)}) async-start(), calls=%async_computation.2 | async-start | bytes 13369344 | tf_op jit(solution)/shard_map/all_gather | solution.py:93
Sparse Core Ops, SparseCore 0:
  726.8 137.3 reduce-scatter.1
  866.5 99.9 all-gather.1
where the time goes:
time: 1120 us; the launch traced here: 1110 us
  matrix products  382 us (34%)
  local copies, waits for them, and re-layouts  360 us (32%)
  waiting for transfers between devices  233 us (21%)
  other arithmetic  121 us (11%)
  between operations  14.4 us (1%)
    reduce_scatter x1, waiting for transfers between devices, body(): lax.psum_scatter(phase_sum(picked, plane_freq, positions, size_x, norm_fa...  137 us
    dot_general x1, matrix products, body(): jnp.einsum('awgk,hk->awgh', left_side, lax.all_gather(owned, 'blk', axis=...  108 us
    all_gather x1, waiting for transfers between devices, body(): lax.all_gather(owned, 'blk', axis=0, tiled=True)  95.6 us
    reduce_sum x1, other arithmetic, phase_sum(): real_m = jnp.sum(real_v * cosine + imag_v * sine, axis=1)  82.4 us
    reshape x1, local copies, waits for them, and re-layouts, plane_picks(): real_b.reshape(size_y * size_z, planes, pair_count)  59.9 us
    reshape x1, local copies, waits for them, and re-layouts, plane_picks(): imag_b.reshape(size_y * size_z, planes, pair_count)  59.8 us
    dot_general x1, matrix products, plane_picks(): jnp.einsum('ly,ykxp->lkxp', cos_y, real_a, precision=highest)  54.9 us
    dot_general x1, matrix products, plane_picks(): jnp.einsum('ly,ykxp->lkxp', sin_y, real_a, precision=highest)  54.7 us
  transfers between devices with their start and end apart: 2, of which 2 were waited for; matrix products, arithmetic and copies ran while one was open for 1% of the time, Pallas kernels for 0%

commit v1 on v0

v1 whole, which is shorter than its diff:
```python
import math

import jax
import jax.numpy as jnp
from jax import lax
from jax.sharding import PartitionSpec as P

high = lax.Precision.HIGH


def dft_tables(rows, length):
    angles = (
        jnp.arange(rows, dtype=jnp.int32)[:, None]
        * jnp.arange(length, dtype=jnp.int32)[None, :]
        % length
    ).astype(jnp.float32) * (2.0 * math.pi / length)
    return (jnp.cos(angles), jnp.sin(angles))


def plane_transform(val_part, cond_part):
    num_val, planes, size_y, size_z = val_part.shape
    num_cond = cond_part.shape[0]
    half = size_z // 2 + 1
    val_t = jnp.transpose(val_part, (1, 3, 2, 0))
    cond_t = jnp.transpose(cond_part, (1, 0, 3, 2))
    density = jnp.concatenate(
        [
            val_t[x] * cond_t[x, c][:, :, None]
            for x in range(planes)
            for c in range(num_cond)
        ],
        axis=2,
    )
    columns = planes * num_cond * num_val
    cos_z, sin_z = dft_tables(half, size_z)
    table_z = jnp.stack([cos_z, -sin_z], axis=1).reshape(2 * half, size_z)
    after_z = jnp.einsum("mz,zyn->myn", table_z, density, precision=high)
    after_z = after_z.reshape(half, 2 * size_y, columns)
    cos_y, sin_y = dft_tables(size_y, size_y)
    table_y = jnp.concatenate(
        [
            jnp.concatenate([cos_y, sin_y], axis=1),
            jnp.concatenate([-sin_y, cos_y], axis=1),
        ],
        axis=0,
    )
    after_y = jnp.einsum("rs,ksn->krn", table_y, after_z, precision=high)
    return after_y.reshape(half * 2 * size_y, columns)


def body(psi_val, psi_cond, e_val, e_cond, occ, freq, gmap):
    num_val, planes, size_y, size_z = psi_val.shape
    num_cond = psi_cond.shape[0]
    pairs = num_val * num_cond
    size_x = planes * lax.axis_size("blk")
    norm_factor = 1.0 / math.sqrt(size_x * size_y * size_z)

    kx = gmap // (size_y * size_z)
    ky = gmap // size_z % size_y
    kz = gmap % size_z
    mirrored = kz > size_z // 2
    row = jnp.where(
        mirrored,
        (size_z - kz) * 2 * size_y + (size_y - ky) % size_y,
        kz * 2 * size_y + ky,
    )
    sign = jnp.where(mirrored, -1.0, 1.0).astype(jnp.float32)[:, None]
    spectrum = plane_transform(psi_val, psi_cond)
    real_v = spectrum.at[row].get(mode="promise_in_bounds")
    imag_v = spectrum.at[row + size_y].get(mode="promise_in_bounds")

    positions = lax.axis_index("blk") * planes + jnp.arange(planes, dtype=jnp.int32)
    angles = (kx[:, None] * positions[None, :] % size_x).astype(jnp.float32) * (
        2.0 * math.pi / size_x
    )
    cosine = jnp.cos(angles) * norm_factor
    sine = jnp.sin(angles) * norm_factor
    real_m = 0.0
    imag_m = 0.0
    for x in range(planes):
        real_x = real_v[:, x * pairs : (x + 1) * pairs]
        imag_x = imag_v[:, x * pairs : (x + 1) * pairs] * sign
        real_m = real_m + real_x * cosine[:, x : x + 1] + imag_x * sine[:, x : x + 1]
        imag_m = imag_m + imag_x * cosine[:, x : x + 1] - real_x * sine[:, x : x + 1]
    owned = lax.psum_scatter(
        jnp.concatenate([real_m, imag_m], axis=1), "blk", scatter_dimension=0, tiled=True
    )
    everyone = lax.all_gather(owned, "blk", axis=0, tiled=True)

    gaps = (e_val[None, :] - e_cond[:, None])[:, :, None]
    weights = (
        occ.astype(jnp.float32)[None, :, None] * gaps / (gaps * gaps + (freq * freq)[None, None, :])
    )
    weights = weights.reshape(pairs, freq.shape[0]) / math.sqrt(pairs)
    freq_weights = jnp.transpose(weights)[:, None, :]
    real_w = owned[None, :, :pairs] * freq_weights
    imag_w = owned[None, :, pairs:] * freq_weights
    chi_real = jnp.einsum(
        "wgk,hk->wgh", jnp.concatenate([real_w, imag_w], axis=2), everyone, precision=high
    )
    chi_imag = jnp.einsum(
        "wgk,hk->wgh", jnp.concatenate([imag_w, -real_w], axis=2), everyone, precision=high
    )
    return (chi_real, chi_imag)


def solution(mesh):
    return jax.shard_map(
        body,
        mesh=mesh,
        in_specs=(
            P("cell", "blk", None, None),
            P("cell", "blk", None, None),
            P("cell"),
            P("cell"),
            P("cell"),
            P("cell"),
            P("cell"),
        ),
        out_specs=(P("cell", "blk", None), P("cell", "blk", None)),
        check_vma=False,
    )
```

time: 1120 us -> 538 us (0.48)
  matrix products: 382 us -> 109 us
  local copies, waits for them, and re-layouts: 360 us -> 104 us
  other arithmetic: 121 us -> 73.9 us
    dot_general x7 -> x4, matrix products: 382 us -> 109 us  [the longest x1 31.1 us: body(): jnp.einsum('wgk,hk->wgh', jnp.concatenate([imag_w, -real_w], axis=2), eve...]
    reshape x2 -> x1, local copies, waits for them, and re-layouts: 120 us -> 0.03 us  [plane_transform(): table_z = jnp.stack([cos_z, -sin_z], axis=1).reshape(2 * half, size_z)]
    reduce_sum x1 -> x0, other arithmetic: 82.4 us -> none  [phase_sum(): real_m = jnp.sum(real_v * cosine + imag_v * sine, axis=1)]
    mul x3 -> x1, local copies, waits for them, and re-layouts: 40.7 us -> 0.96 us  [plane_transform(): val_t[x] * cond_t[x, c][:, :, None]]
    gather x2, local copies, waits for them, and re-layouts: 107 us -> 71.1 us  [the longest x1 35.6 us: body(): imag_v = spectrum.at[row + size_y].get(mode='promise_in_bounds')]
    mul x4 -> x2, other arithmetic: 34.1 us -> 0.67 us  [the longest x1 0.6 us: body(): cosine = jnp.cos(angles) * norm_factor]
    squeeze x1 -> x0, local copies, waits for them, and re-layouts: 28.8 us -> none  [body(): return (chi_both[0], chi_both[1])]
    dot_general x0 -> x1, local copies, waits for them, and re-layouts: none -> 25.8 us  [plane_transform(): after_z = jnp.einsum('mz,zyn->myn', table_z, density, precision=high)]
where the time goes in v1:
time: 538 us
  waiting for transfers between devices  236 us (44%)
  matrix products  109 us (20%)
  local copies, waits for them, and re-layouts  104 us (19%)
  other arithmetic  73.9 us (14%)
  between operations  14.2 us (3%)
    reduce_scatter x1, waiting for transfers between devices, body(): lax.psum_scatter(jnp.concatenate([real_m, imag_m], axis=1), 'blk', scatte...  138 us
    all_gather x1, waiting for transfers between devices, body(): everyone = lax.all_gather(owned, 'blk', axis=0, tiled=True)  98.3 us
    gather x1, local copies, waits for them, and re-layouts, body(): imag_v = spectrum.at[row + size_y].get(mode='promise_in_bounds')  35.6 us
    gather x1, local copies, waits for them, and re-layouts, body(): real_v = spectrum.at[row].get(mode='promise_in_bounds')  35.5 us
    dot_general x1, matrix products, body(): jnp.einsum('wgk,hk->wgh', jnp.concatenate([imag_w, -real_w], axis=2), eve...  31.1 us
    dot_general x1, matrix products, body(): jnp.einsum('wgk,hk->wgh', jnp.concatenate([real_w, imag_w], axis=2), ever...  28.1 us
    dot_general x1, local copies, waits for them, and re-layouts, plane_transform(): after_z = jnp.einsum('mz,zyn->myn', table_z, density, precision=high)  25.8 us
    dot_general x1, matrix products, plane_transform(): after_y = jnp.einsum('rs,ksn->krn', table_y, after_z, precision=high)  25.4 us
  transfers between devices with their start and end apart: 2, of which 2 were waited for; matrix products, arithmetic and copies ran while one was open for 1% of the time, Pallas kernels for 0%

profile of v1, /device:TPU:0, one launch (start us, length us, event | category | flops | bytes accessed | tf_op | source)
XLA Modules:
  0.0 537.6 jit_solution(1454509144264351076)
XLA Ops:
  7.2 0.5 sine_negate_fusion
  8.0 1.4 fusion.38
  9.4 1.3 broadcast_select_fusion
  10.7 1.0 slice_bitcast_fusion.4
  11.8 3.2 multiply_dynamic-update-slice_fusion.11
  15.0 3.7 multiply_dynamic-update-slice_fusion.10
  18.7 1.8 multiply_dynamic-update-slice_fusion.9
  20.4 1.9 multiply_dynamic-update-slice_fusion.8
  22.3 1.8 multiply_dynamic-update-slice_fusion.7
  24.1 1.7 multiply_dynamic-update-slice_fusion.6
  25.9 1.8 multiply_dynamic-update-slice_fusion.5
  27.6 1.7 multiply_dynamic-update-slice_fusion.4
  29.4 1.8 multiply_dynamic-update-slice_fusion.3
  31.1 1.9 multiply_dynamic-update-slice_fusion.2
  33.0 1.9 multiply_dynamic-update-slice_fusion.1
  34.9 1.8 multiply_dynamic-update-slice_fusion
  36.8 24.7 %fusion.21 = f32[66,64,1536]{2,0,1:T(8,128)} fusion(f32[64,64,1536]{2,0,1:T(8,128)} %multiply_dynamic-update-slice_fusion, f32[66,64]{1,0:T(8,128)S(1)} %reshape.165), kind=kOutput, calls=%fused_computation.64 | convolution fusion | flops 2491416576 | bytes 51134976 | tf_op jit(solution)/shard_map/mz,zyn->myn/dot_general | solution.py:37
  61.4 25.8 %copy.10 = f32[66,64,1536]{2,1,0:T(8,128)} copy(f32[66,64,1536]{2,0,1:T(8,128)} %fusion.21) | data formatting | bytes 51904512 | tf_op jit(solution)/shard_map/mz,zyn->myn/dot_general | solution.py:37
  87.3 25.4 %fusion.14 = f32[33,1536,128]{1,2,0:T(8,128)} fusion(f32[33,128,1536]{2,1,0:T(8,128)} %bitcast.99, f32[64,64]{1,0:T(8,128)S(1)} %get-tuple-element.37, f32[64,64]{1,0:T(8,128)S(1)} %fusion.43, f32[64,64]{1,0:T(8,128)S(1)} %get-tuple-element.36), kind=kOutput, calls=%fused_computation.50 | convolution fusion | flops 4982882304 | bytes 51953664 | tf_op jit(solution)/shard_map/rs,ksn->krn/dot_general | solution.py:47
  112.7 35.5 %gather_fusion = f32[4096,1536]{1,0:T(8,128)} fusion(f32[4224,1536]{1,0:T(8,128)} %bitcast.97, s32[4096]{0:T(1024)S(1)} %fusion.37), kind=kCustom, calls=%fused_computation | custom fusion | bytes 50348032 | tf_op jit(solution)/shard_map/gather | solution.py:69
  148.2 35.6 %gather_fusion.1 = f32[4096,1536]{1,0:T(8,128)} fusion(f32[4224,1536]{1,0:T(8,128)} %bitcast.98, s32[4096]{0:T(1024)S(1)} %get-tuple-element.2), kind=kCustom, calls=%fused_computation.1 | custom fusion | bytes 50348032 | tf_op jit(solution)/shard_map/gather | solution.py:70
  183.8 0.6 cosine_multiply_fusion
  184.5 20.2 %multiply_add_fusion = f32[4096,384]{1,0:T(8,128)} fusion(f32[4096,1536]{1,0:T(8,128)} %gather_fusion, f32[4096,1536]{1,0:T(8,128)} %gather_fusion.1, f32[4096]{0:T(1024)S(1)} %bitcast.125, f32[4096]{0:T(1024)S(1)} %bitcast.115, f32[4096]{0:T(1024)S(1)} %bitcast.123, f32[4096]{0:T(1024)S(1)} %bitcast.117, f32[4096]{0:T(1024)S(1)} %bitcast.121, ...), kind=kLoop, calls=%fused_computation.12 | loop fusion | flops 29884416 | bytes 56770560 | tf_op jit(solution)/shard_map/add | solution.py:83
  204.7 5.0 copy-done
  209.7 11.7 %multiply_subtract_fusion = f32[4096,384]{1,0:T(8,128)} fusion(f32[4096,1536]{1,0:T(8,128)S(1)} %copy-done, f32[4096,1536]{1,0:T(8,128)} %gather_fusion.1, f32[4096]{0:T(1024)S(1)} %bitcast.126, f32[4096]{0:T(1024)S(1)} %bitcast.116, f32[4096]{0:T(1024)S(1)} %bitcast.124, f32[4096]{0:T(1024)S(1)} %bitcast.118, f32[4096]{0:T(1024)S(1)} %bitcast.122, ...), kind=kLoop, calls=%fused_computation.11 | loop fusion | flops 29884416 | bytes 56770560 | tf_op jit(solution)/shard_map/sub | solution.py:84
  221.4 10.3 %pad_maximum_fusion = f32[4096,768]{1,0:T(8,128)} fusion(f32[4096,384]{1,0:T(8,128)} %multiply_subtract_fusion, f32[4096,384]{1,0:T(8,128)} %multiply_add_fusion), kind=kLoop, calls=%fused_computation.2 | loop fusion | flops 3145728 | bytes 25165824 | tf_op jit(solution)/shard_map/concatenate | solution.py:86
  231.8 137.5 %reduce-scatter.2.cloned.1.call-done = f32[256,768]{1,0:T(8,128)} async-done(((f32[4096,768]{1,0:T(8,128)}), f32[256,768]{1,0:T(8,128)}) %reduce-scatter.2.cloned.1.call-update) | async-done | bytes 786448 | tf_op jit(solution)/shard_map/reduce_scatter | solution.py:85
  369.6 1.2 fusion.52
  370.8 2.5 fusion.10
  373.2 98.3 %all-gather.2.cloned.1.call-done = f32[4096,768]{1,0:T(8,128)} async-done(((f32[256,768]{1,0:T(8,128)}), f32[4096,768]{1,0:T(8,128)}) %all-gather.2.cloned.1.call-update) | async-done | bytes 12582928 | tf_op jit(solution)/shard_map/all_gather | solution.py:88
  471.5 31.1 %fusion = f32[5,256,4096]{2,1,0:T(8,128)} fusion(f32[4096,768]{1,0:T(8,128)} %all-gather.2.cloned.1.call-done, f32[5,256,384]{2,1,0:T(8,128)} %get-tuple-element.6, f32[5,256,384]{2,1,0:T(8,128)} %get-tuple-element.31), kind=kOutput, calls=%fused_computation.3 | convolution fusion | flops 24160174080 | bytes 37486592 | tf_op jit(solution)/shard_map/wgk,hk->wgh/dot_general | solution.py:101
  502.6 28.1 %fusion.2 = f32[5,256,4096]{2,1,0:T(8,128)} fusion(f32[4096,768]{1,0:T(8,128)S(1)} %copy-done.7, f32[5,256,384]{2,1,0:T(8,128)S(1)} %copy-done.2, f32[5,256,384]{2,1,0:T(8,128)S(1)} %get-tuple-element.7), kind=kOutput, calls=%fused_computation.5 | convolution fusion | flops 24160174080 | bytes 37486592 | tf_op jit(solution)/shard_map/wgk,hk->wgh/dot_general | solution.py:98
  (35 shorter events, 0.8 us)
Async XLA Ops:
  7.2 362.2 %reduce-scatter.2.cloned.1.call-start = ((), (), s32[]{:S(2)}) async-start(), calls=%async_computation.1 | async-start | bytes 13369344 | tf_op jit(solution)/shard_map/reduce_scatter | solution.py:85
  11.8 6.9 %copy-start.1 = (f32[128,4,64,64]{0,3,2,1:T(8,128)S(1)}, f32[128,4,64,64]{0,3,2,1:T(8,128)}, u32[]{:S(2)}) copy-start(f32[128,4,64,64]{0,3,2,1:T(8,128)} %param.7) | copy-start | bytes 25165828
  148.2 35.6 %copy-start.4 = (s32[4096]{0:T(1024)S(1)}, s32[4096]{0:T(1024)}, u32[]{:S(2)}) copy-start(s32[4096]{0:T(1024)} %get-tuple-element.30) | copy-start | bytes 49156
  148.2 36.3 %copy-start.3 = (f32[4096]{0:T(1024)S(1)}, f32[4096]{0:T(1024)}, u32[]{:S(2)}) copy-start(f32[4096]{0:T(1024)} %broadcast_select_fusion) | copy-start | bytes 49156
  184.5 25.2 %copy-start = (f32[4096,1536]{1,0:T(8,128)S(1)}, f32[4096,1536]{1,0:T(8,128)}, u32[]{:S(2)}) copy-start(f32[4096,1536]{1,0:T(8,128)} %gather_fusion) | copy-start | bytes 75497472
  231.7 137.6 %copy-start.8 = (s32[128]{0:T(128)S(1)}, s32[128]{0:T(128)}, u32[]{:S(2)}) copy-start(s32[128]{0:T(128)} %param.11) | copy-start | bytes 1540
  231.7 137.7 %copy-start.9 = (f32[5]{0:T(128)S(1)}, f32[5]{0:T(128)}, u32[]{:S(2)}) copy-start(f32[5]{0:T(128)} %param.12) | copy-start | bytes 64
  231.7 137.7 %copy-start.5 = (f32[128]{0:T(128)S(1)}, f32[128]{0:T(128)}, u32[]{:S(2)}) copy-start(f32[128]{0:T(128)} %param.9) | copy-start | bytes 1540
  231.7 137.7 %copy-start.6 = (f32[3]{0:T(128)S(1)}, f32[3]{0:T(128)}, u32[]{:S(2)}) copy-start(f32[3]{0:T(128)} %param.10) | copy-start | bytes 40
  231.7 239.8 %all-gather.2.cloned.1.call-start = ((), (), s32[]{:S(2)}) async-start(), calls=%async_computation.2 | async-start | bytes 13369344 | tf_op jit(solution)/shard_map/all_gather | solution.py:88
  471.5 31.1 %copy-start.2 = (f32[5,256,384]{2,1,0:T(8,128)S(1)}, f32[5,256,384]{2,1,0:T(8,128)}, u32[]{:S(2)}) copy-start(f32[5,256,384]{2,1,0:T(8,128)} %get-tuple-element.31) | copy-start | bytes 5898244
  471.5 31.1 %copy-start.7 = (f32[4096,768]{1,0:T(8,128)S(1)}, f32[4096,768]{1,0:T(8,128)}, u32[]{:S(2)}) copy-start(f32[4096,768]{1,0:T(8,128)} %all-gather.2.cloned.1.call-done) | copy-start | bytes 37748740
Sparse Core Ops, SparseCore 0:
  231.9 137.4 reduce-scatter.1
  371.6 99.8 all-gather.1
